TPU v7x, 32 devices: a whole 2x2x4 slice. The times are simulated.
32 devices in a mesh: groups: 2 (over y), gx: 4 (over z), gy: 2 (over x), sa: 2 (over core).
Axes of the slice: x: 2, y: 2, z: 4, core: 2. Of those that a mesh axis runs over, the one named last changes fastest.
Arguments:
- source_now: float32 [4, 128, 48, 128], P(('groups', 'sa'), 'gx', 'gy'), parts along dimension 0, may hold values from -6 to 6
- source_later: float32 [4, 128, 48, 128], P(('groups', 'sa'), 'gx', 'gy'), parts along dimension 0, may hold values from -6 to 6
- receiver_now: float32 [4, 128, 48, 128], P(('groups', 'sa'), 'gx', 'gy'), parts along dimension 0, may hold values from -6 to 6
- receiver_later: float32 [4, 128, 48, 128], P(('groups', 'sa'), 'gx', 'gy'), parts along dimension 0, may hold values from -6 to 6
- courant: float32 [128, 48, 128], P('gx', 'gy'), may hold values from 0.05 to 0.19
- wavelet: float32 [4, 12], P(('groups', 'sa')), parts along dimension 0, may hold values from -8 to 8
- traces: float32 [4, 12, 64], P(('groups', 'sa')), parts along dimension 0, may hold values from -6 to 6
- source_inline: int32 [4], P(('groups', 'sa')), parts along dimension 0, may hold values from 0 to 127
- source_crossline: int32 [4], P(('groups', 'sa')), parts along dimension 0, may hold values from 0 to 47
- receiver_inline: int32 [4, 64], P(('groups', 'sa')), parts along dimension 0, may hold values from 0 to 127
- receiver_crossline: int32 [4, 64], P(('groups', 'sa')), parts along dimension 0, may hold values from 0 to 47
Outputs:
- source_first: float32 [4, 128, 48, 128], P(('groups', 'sa'), 'gx', 'gy'), parts along dimension 0
- source_second: float32 [4, 128, 48, 128], P(('groups', 'sa'), 'gx', 'gy'), parts along dimension 0
- receiver_first: float32 [4, 128, 48, 128], P(('groups', 'sa'), 'gx', 'gy'), parts along dimension 0
- receiver_second: float32 [4, 128, 48, 128], P(('groups', 'sa'), 'gx', 'gy'), parts along dimension 0
- image_stack: float32 [256, 48, 128], P(('groups', 'gx', 'sa'), 'gy'), parts along dimension 0
There are 2 independent parts, one for each index of `groups`. A program takes and returns all parts, laid end to end along the dimension named above; an argument that names none is the same for every part. Nothing has to cross between parts.
All inputs are finite; a program needn't handle non-finite values.
Results may differ from a plain program's by a relative error of at most 0.0003.
Values sent between devices are 32-bit elements; how exact they have to be, the bound alone decides.
A program may use at most 128 MiB of HBM per device.

v0:
```python
import functools

import jax
import jax.numpy as jnp
from jax import lax
from jax.experimental import pallas as pl
from jax.experimental.pallas import tpu as pltpu
from jax.sharding import PartitionSpec as P

SRC_DEPTH = 3
REC_DEPTH = 2
STEPS = 12
REACH = 4
SIDE = 8
PLANES = 4

COEFFS = (-205.0 / 72.0, 8.0 / 5.0, -1.0 / 5.0, 8.0 / 315.0, -1.0 / 560.0)
MESH = pl.DeviceIdType.MESH
BF16 = jnp.bfloat16
F32 = jnp.float32


def halves(values):
    high = values.astype(BF16)
    low = (values - high.astype(F32)).astype(BF16)
    return high, low


def kernel(
    s_now, s_later, r_now, r_later, speed_in,
    wave, traces, s_in, s_cr, r_in, r_cr,
    s_first, s_second, r_first, r_second, image,
    s0, s1, r0, r1, speed, corr, other, mine, q_s, q_r, w_main, w_side,
    x_out, x_in, load_sem, send_sem, recv_sem, sum_sem, store_sem,
):
    ni, nc, nz = speed.shape
    cells = ni * nc
    half = ni // 2
    gx, gy, sa = lax.axis_index("gx"), lax.axis_index("gy"), lax.axis_index("sa")
    last_x, last_y = lax.axis_size("gx") - 1, lax.axis_size("gy") - 1
    below, above = gx > 0, gx < last_x
    left, right = gy > 0, gy < last_y
    fields = ((s0, s1), (r0, r1))
    rows = pl.ds(SIDE, nc)
    inner = (pl.ds(REACH, ni), rows)

    loads = [
        pltpu.make_async_copy(src, dst, load_sem.at[n])
        for n, (src, dst) in enumerate(
            (
                (s_now, s0.at[inner]),
                (r_now, r0.at[inner]),
                (s_later, s1.at[inner]),
                (r_later, r1.at[inner]),
                (speed_in, speed),
            )
        )
    ]
    for load in loads:
        load.start()

    ways = (
        ({"gx": gx - 1}, below, above),
        ({"gx": gx + 1}, above, below),
        ({"gy": gy - 1}, left, right),
        ({"gy": gy + 1}, right, left),
    )
    barrier = pltpu.get_barrier_semaphore()
    for target, sends, _ in ways:
        @pl.when(sends)
        def _():
            pl.semaphore_signal(barrier, inc=1, device_id=target, device_id_type=MESH)
    pl.semaphore_signal(barrier, inc=1, device_id={"sa": 1 - sa}, device_id_type=MESH)

    def exchange(field, slot, way):
        buf = fields[field][slot]
        if way == 0:
            src, dst = buf.at[pl.ds(REACH, REACH), rows], buf.at[pl.ds(REACH + ni, REACH), rows]
        elif way == 1:
            src, dst = buf.at[pl.ds(ni, REACH), rows], buf.at[pl.ds(0, REACH), rows]
        else:
            src, dst = x_out.at[field, slot, way - 2], x_in.at[field, slot, way - 2]
        return pltpu.make_async_remote_copy(
            src_ref=src, dst_ref=dst,
            send_sem=send_sem.at[field, slot, way], recv_sem=recv_sem.at[field, slot, way],
            device_id=ways[way][0], device_id_type=MESH,
        )

    def send(field, slot):
        buf = fields[field][slot]
        for way in (2, 3, 0, 1):
            @pl.when(ways[way][1])
            def _():
                if way == 2:
                    x_out[field, slot, 0] = buf[REACH:REACH + ni, SIDE:SIDE + REACH, :]
                if way == 3:
                    x_out[field, slot, 1] = buf[REACH:REACH + ni, SIDE + nc - REACH:SIDE + nc, :]
                exchange(field, slot, way).start()

    def sent(field, slot):
        for way in range(4):
            @pl.when(ways[way][1])
            def _():
                exchange(field, slot, way).wait_send()

    def receive(field, slot):
        buf = fields[field][slot]
        for way in (2, 3, 0, 1):
            @pl.when(ways[way][2])
            def _():
                exchange(field, slot, way).wait_recv()
                if way == 2:
                    buf[REACH:REACH + ni, SIDE + nc:SIDE + nc + REACH, :] = x_in[field, slot, 0]
                if way == 3:
                    buf[REACH:REACH + ni, SIDE - REACH:SIDE, :] = x_in[field, slot, 1]

    for pair in fields:
        for buf in pair:
            @pl.when(jnp.logical_not(below))
            def _():
                buf[0:REACH, SIDE:SIDE + nc, :] = jnp.zeros((REACH, nc, nz), F32)
            @pl.when(jnp.logical_not(above))
            def _():
                buf[REACH + ni:, SIDE:SIDE + nc, :] = jnp.zeros((REACH, nc, nz), F32)
            @pl.when(jnp.logical_not(left))
            def _():
                buf[REACH:REACH + ni, SIDE - REACH:SIDE, :] = jnp.zeros((ni, REACH, nz), F32)
            @pl.when(jnp.logical_not(right))
            def _():
                buf[REACH:REACH + ni, SIDE + nc:SIDE + nc + REACH, :] = jnp.zeros((ni, REACH, nz), F32)

    peers = 1
    for _, sends, _ in ways:
        peers = peers + sends.astype(jnp.int32)
    pl.semaphore_wait(barrier, peers)
    loads[0].wait()
    send(0, 0)
    loads[1].wait()
    send(1, 0)

    line = lax.broadcasted_iota(jnp.int32, (nz, nz), 0)
    lane = lax.broadcasted_iota(jnp.int32, (nz, nz), 1)
    apart = jnp.abs(line - lane)
    band = jnp.where(apart == 0, 3.0 * COEFFS[0], 0.0)
    for distance in range(1, 5):
        band = jnp.where(apart == distance, COEFFS[distance], band)
    band_high, band_low = halves(band.astype(F32))
    w_main[0:nz, :] = band_high
    w_main[nz:, :] = band_high
    for field in range(2):
        w_side[field, 0:nz, :] = band_low

    pick = (lax.broadcasted_iota(jnp.int32, (nz, STEPS), 0) % 32
            == lax.broadcasted_iota(jnp.int32, (nz, STEPS), 1)).astype(F32)
    dot = functools.partial(lax.dot_general, precision=lax.Precision.HIGHEST, preferred_element_type=F32)
    by_lane = dot(pick, traces[0], (((1,), (0,)), ((), ())))
    wave_lane = dot(jnp.broadcast_to(wave[...], (8, STEPS)), pick, (((1,), (1,)), ((), ())))[0:1]

    def local(inline, cross):
        a, b = inline - gx * ni, cross - gy * nc
        inside = (a >= 0) & (a < ni) & (b >= 0) & (b < nc)
        return jnp.where(inside, a * nc + b, -1)

    where_r = local(r_in[...], r_cr[...])
    where_s = local(s_in[0], s_cr[0])
    part = PLANES * nc

    def terms(total):
        group = lax.broadcasted_iota(jnp.int32, (part, nz), 1) // 32
        first = total.astype(BF16).astype(F32)
        rest = total - first
        second = rest.astype(BF16).astype(F32)
        third = rest - second
        return jnp.where(group == 0, first, jnp.where(group == 1, second, jnp.where(group == 2, third, 0.0))).astype(BF16)

    @pl.loop(0, cells // part)
    def _(n):
        start = pl.multiple_of(n * part, part)
        index = lax.broadcasted_iota(jnp.int32, (part, 1), 0) + start
        hot = (index == where_r).astype(F32)
        q_r[pl.ds(start, part), :] = terms(dot(hot, by_lane, (((1,), (1,)), ((), ()))))
        q_s[pl.ds(start, part), :] = terms(jnp.where(index == where_s, wave_lane, 0.0))

    corr[...] = jnp.zeros_like(corr)
    for load in loads[2:]:
        load.wait()

    mul = functools.partial(jnp.dot, preferred_element_type=F32)

    def advance(field, slot, moment):
        cur, new = fields[field][slot], fields[field][1 - slot]
        depth = (SRC_DEPTH, REC_DEPTH)[field]
        q = (q_s, q_r)[field]
        spot = (line < 96) & (line % 32 == moment) & (lane == depth)
        w_side[field, nz:, :] = spot.astype(F32).astype(BF16)
        main, side = w_main[...], w_side[field]
        for low in range(0, ni, PLANES):
            at = low + REACH
            here = slice(at, at + PLANES)
            centre = cur[here, SIDE:SIDE + nc, :]
            high_part, low_part = halves(centre.reshape(part, nz))
            total = mul(jnp.concatenate([high_part, low_part], axis=1), main)
            total = total + mul(
                jnp.concatenate([high_part, q[low * nc:low * nc + part, :]], axis=1), side
            )
            total = total.reshape(PLANES, nc, nz)
            for k in range(1, 5):
                around = (
                    cur[at + k:at + k + PLANES, SIDE:SIDE + nc, :]
                    + cur[at - k:at - k + PLANES, SIDE:SIDE + nc, :]
                ) + (cur[here, SIDE + k:SIDE + k + nc, :] + cur[here, SIDE - k:SIDE - k + nc, :])
                total = total + COEFFS[k] * around
            fresh = 2.0 * centre - new[here, SIDE:SIDE + nc, :] + speed[low:low + PLANES] * total
            new[here, SIDE:SIDE + nc, :] = fresh
            if field == 1:
                corr[low:low + PLANES] += fresh * s_at(slot)[here, SIDE:SIDE + nc, :]

    def s_at(slot):
        return fields[0][1 - slot]

    @pl.loop(0, STEPS // 2)
    def _(pair):
        for slot in range(2):
            for field in range(2):
                receive(field, slot)
                if slot == 0:
                    @pl.when(pair > 0)
                    def _():
                        sent(field, 1)
                else:
                    sent(field, 0)
                advance(field, slot, 2 * pair + slot)
                if slot == 0:
                    send(field, 1)
                else:
                    @pl.when(pair < STEPS // 2 - 1)
                    def _():
                        send(field, 0)

    theirs = pl.ds((1 - sa) * half, half)
    own = pl.ds(sa * half, half)
    swap = pltpu.make_async_remote_copy(
        src_ref=corr.at[theirs], dst_ref=other, send_sem=sum_sem.at[0], recv_sem=sum_sem.at[1],
        device_id={"sa": 1 - sa}, device_id_type=MESH,
    )
    swap.start()
    stores = [
        pltpu.make_async_copy(src.at[inner], dst, store_sem.at[n])
        for n, (src, dst) in enumerate(((s0, s_first), (s1, s_second), (r0, r_first), (r1, r_second)))
    ]
    for store in stores:
        store.start()
    sent(0, 1)
    sent(1, 1)
    swap.wait()
    mine[...] = (corr[own] + other[...]) * (1.0 / STEPS)
    last = pltpu.make_async_copy(mine, image, store_sem.at[4])
    last.start()
    for store in stores:
        store.wait()
    last.wait()


def body(s_now, s_later, r_now, r_later, courant, wave, traces, s_in, s_cr, r_in, r_cr):
    ni, nc, nz = courant.shape
    half = ni // 2
    wide = (ni + 2 * REACH, nc + 2 * SIDE, nz)
    hbm = pl.BlockSpec(memory_space=pl.ANY)
    vmem = pl.BlockSpec(memory_space=pltpu.VMEM)
    smem = pl.BlockSpec(memory_space=pltpu.SMEM)
    tile = jax.ShapeDtypeStruct((ni, nc, nz), F32)
    outs = pl.pallas_call(
        kernel,
        out_shape=[tile] * 4 + [jax.ShapeDtypeStruct((half, nc, nz), F32)],
        in_specs=[hbm] * 5 + [vmem] * 2 + [smem] * 2 + [vmem] * 2,
        out_specs=[hbm] * 5,
        scratch_shapes=[pltpu.VMEM(wide, F32)] * 4
        + [
            pltpu.VMEM((ni, nc, nz), F32),
            pltpu.VMEM((ni, nc, nz), F32),
            pltpu.VMEM((half, nc, nz), F32),
            pltpu.VMEM((half, nc, nz), F32),
            pltpu.VMEM((ni * nc, nz), BF16),
            pltpu.VMEM((ni * nc, nz), BF16),
            pltpu.VMEM((2 * nz, nz), BF16),
            pltpu.VMEM((2, 2 * nz, nz), BF16),
            pltpu.VMEM((2, 2, 2, ni, REACH, nz), F32),
            pltpu.VMEM((2, 2, 2, ni, REACH, nz), F32),
            pltpu.SemaphoreType.DMA((5,)),
            pltpu.SemaphoreType.DMA((2, 2, 4)),
            pltpu.SemaphoreType.DMA((2, 2, 4)),
            pltpu.SemaphoreType.DMA((2,)),
            pltpu.SemaphoreType.DMA((5,)),
        ],
        compiler_params=pltpu.CompilerParams(
            collective_id=0, has_side_effects=True, vmem_limit_bytes=62 * 1024 * 1024
        ),
        name="window",
    )(s_now[0], s_later[0], r_now[0], r_later[0], courant, wave, traces, s_in, s_cr, r_in, r_cr)
    return tuple(out[None] for out in outs[:4]) + (outs[4],)


def solution(mesh):
    field = P(("groups", "sa"), "gx", "gy", None)
    in_specs = (
        (field,) * 4
        + (P("gx", "gy", None), P(("groups", "sa"), None), P(("groups", "sa"), None, None))
        + (P(("groups", "sa")),) * 2
        + (P(("groups", "sa"), None),) * 2
    )
    out_specs = (field,) * 4 + (P(("groups", "gx", "sa"), "gy", None),)
    return jax.shard_map(body, mesh=mesh, in_specs=in_specs, out_specs=out_specs, check_vma=False)
```

profile of v0, /device:TPU:0, one launch (start us, length us, event | category | flops | bytes accessed | tf_op | source)
XLA Modules:
  0.0 67.2 jit_solution(4289271569932486232)
XLA Ops:
  0.6 0.0 copy-start.4
  1.9 0.0 copy-done.4
  2.0 0.6 copy.16.traces
  2.6 58.8 %window.1 = (f32[32,24,128]{2,1,0:T(8,128)}, f32[32,24,128]{2,1,0:T(8,128)}, f32[32,24,128]{2,1,0:T(8,128)}, f32[32,24,128]{2,1,0:T(8,128)}, f32[16,24,128]{2,1,0:T(8,128)}) custom-call(f32[32,24,128]{2,1,0:T(8,128)} %bitcast.8, f32[32,24,128]{2,1,0:T(8,128)} %bitcast.9, f32[32,24,128]{2,1,0:T(8,128)} %bitcast.10, f32[32,24,128]{2,1,0:T(8,128)} %bitcast.11, ...), custom_call_target="tpu_custom_call" | custom-call | tf_op jit(solution)/shard_map/window/pallas_call | solution.py:272
  61.3 0.0 copy-start.2
  61.4 1.8 %copy.24 = f32[1,32,24,128]{3,2,1,0:T(8,128)} copy(f32[1,32,24,128]{3,2,1,0:T(8,128)} %bitcast.15) | data formatting | bytes 786432
  63.2 0.0 copy-done.2
  63.2 0.0 copy-start.1
  63.2 0.7 %copy.25 = f32[1,32,24,128]{3,2,1,0:T(8,128)} copy(f32[1,32,24,128]{3,2,1,0:T(8,128)S(1)} %bitcast.14) | data formatting | bytes 786432
  63.9 0.4 copy-done.1
  64.3 0.0 copy-start
  64.3 0.7 %copy.26 = f32[1,32,24,128]{3,2,1,0:T(8,128)} copy(f32[1,32,24,128]{3,2,1,0:T(8,128)S(1)} %bitcast.13) | data formatting | bytes 786432
  65.1 0.4 copy-done
  65.5 0.0 copy-start.3
  65.5 0.7 %copy.27 = f32[1,32,24,128]{3,2,1,0:T(8,128)} copy(f32[1,32,24,128]{3,2,1,0:T(8,128)S(1)} %bitcast.12) | data formatting | bytes 786432
  66.2 0.3 copy-done.3
  66.5 0.7 %copy.28 = f32[16,24,128]{2,1,0:T(8,128)} copy(f32[16,24,128]{2,1,0:T(8,128)S(1)} %copy-done.3) | data formatting | bytes 393216
Async XLA Ops:
  0.6 1.3 %copy-start.4 = (f32[1,12,64]{2,0,1:T(1,128)S(1)}, f32[1,12,64]{2,0,1:T(1,128)}, u32[]{:S(2)}) copy-start(f32[1,12,64]{2,0,1:T(1,128)} %param.17) | copy-start | bytes 9220
  61.3 1.8 %copy-start.2 = (f32[32,24,128]{2,1,0:T(8,128)S(1)}, f32[32,24,128]{2,1,0:T(8,128)}, u32[]{:S(2)}) copy-start(f32[32,24,128]{2,1,0:T(8,128)} %get-tuple-element.11) | copy-start | bytes 1179652
  63.2 1.1 %copy-start.1 = (f32[32,24,128]{2,1,0:T(8,128)S(1)}, f32[32,24,128]{2,1,0:T(8,128)}, u32[]{:S(2)}) copy-start(f32[32,24,128]{2,1,0:T(8,128)} %get-tuple-element.12) | copy-start | bytes 1179652
  64.3 1.1 %copy-start = (f32[32,24,128]{2,1,0:T(8,128)S(1)}, f32[32,24,128]{2,1,0:T(8,128)}, u32[]{:S(2)}) copy-start(f32[32,24,128]{2,1,0:T(8,128)} %get-tuple-element.13) | copy-start | bytes 1179652
  65.5 1.1 %copy-start.3 = (f32[16,24,128]{2,1,0:T(8,128)S(1)}, f32[16,24,128]{2,1,0:T(8,128)}, u32[]{:S(2)}) copy-start(f32[16,24,128]{2,1,0:T(8,128)} %get-tuple-element.24) | copy-start | bytes 589828
where the time goes:
time: 67.5 us; the launch traced here: 67.2 us
  Pallas kernels  58.8 us (87%)
  local copies, waits for them, and re-layouts  6.44 us (10%)
  between operations  1.97 us (3%)
    pallas_call x1, Pallas kernels, body(): pl.pallas_call(kernel, out_shape=[tile] * 4 + [jax.ShapeDtypeStruct((half...  58.8 us
    unnamed x16, local copies, waits for them, and re-layouts  6.44 us

commit v1 on v0

--- a/solution.py
+++ b/solution.py
@@ -30,7 +30,7 @@
     s_now, s_later, r_now, r_later, speed_in,
     wave, traces, s_in, s_cr, r_in, r_cr,
     s_first, s_second, r_first, r_second, image,
-    s0, s1, r0, r1, speed, corr, other, mine, q_s, q_r, w_main, w_side,
+    s0, s1, r0, r1, speed, corr, other, mine, factors, weight, product, records,
     x_out, x_in, load_sem, send_sem, recv_sem, sum_sem, store_sem,
 ):
     ni, nc, nz = speed.shape
@@ -141,19 +141,21 @@
     line = lax.broadcasted_iota(jnp.int32, (nz, nz), 0)
     lane = lax.broadcasted_iota(jnp.int32, (nz, nz), 1)
     apart = jnp.abs(line - lane)
-    band = jnp.where(apart == 0, 3.0 * COEFFS[0], 0.0)
+    band = jnp.zeros((nz, nz), F32)
     for distance in range(1, 5):
         band = jnp.where(apart == distance, COEFFS[distance], band)
-    band_high, band_low = halves(band.astype(F32))
-    w_main[0:nz, :] = band_high
-    w_main[nz:, :] = band_high
+    band_high, band_low = halves(band)
     for field in range(2):
-        w_side[field, 0:nz, :] = band_low
+        weight[field, 0:nz, :] = band_high
+        weight[field, nz:2 * nz, :] = band_high
+        weight[field, 2 * nz:3 * nz, :] = band_low
 
     pick = (lax.broadcasted_iota(jnp.int32, (nz, STEPS), 0) % 32
             == lax.broadcasted_iota(jnp.int32, (nz, STEPS), 1)).astype(F32)
     dot = functools.partial(lax.dot_general, precision=lax.Precision.HIGHEST, preferred_element_type=F32)
-    by_lane = dot(pick, traces[0], (((1,), (0,)), ((), ())))
+    for t in range(STEPS):
+        records[t:t + 1, :] = traces[t]
+    by_lane = dot(pick, records[...], (((1,), (0,)), ((), ())))
     wave_lane = dot(jnp.broadcast_to(wave[...], (8, STEPS)), pick, (((1,), (1,)), ((), ())))[0:1]
 
     def local(inline, cross):
@@ -178,64 +180,102 @@
         start = pl.multiple_of(n * part, part)
         index = lax.broadcasted_iota(jnp.int32, (part, 1), 0) + start
         hot = (index == where_r).astype(F32)
-        q_r[pl.ds(start, part), :] = terms(dot(hot, by_lane, (((1,), (1,)), ((), ()))))
-        q_s[pl.ds(start, part), :] = terms(jnp.where(index == where_s, wave_lane, 0.0))
+        factors[1, pl.ds(start, part), 3 * nz:] = terms(dot(hot, by_lane, (((1,), (1,)), ((), ()))))
+        factors[0, pl.ds(start, part), 3 * nz:] = terms(jnp.where(index == where_s, wave_lane, 0.0))
 
     corr[...] = jnp.zeros_like(corr)
     for load in loads[2:]:
         load.wait()
 
-    mul = functools.partial(jnp.dot, preferred_element_type=F32)
-
-    def advance(field, slot, moment):
+    def depth(field, slot, moment):
         cur, new = fields[field][slot], fields[field][1 - slot]
-        depth = (SRC_DEPTH, REC_DEPTH)[field]
-        q = (q_s, q_r)[field]
-        spot = (line < 96) & (line % 32 == moment) & (lane == depth)
-        w_side[field, nz:, :] = spot.astype(F32).astype(BF16)
-        main, side = w_main[...], w_side[field]
+        level = (SRC_DEPTH, REC_DEPTH)[field]
+        spot = (line < 96) & (line % 32 == moment) & (lane == level)
+        weight[field, 3 * nz:, :] = spot.astype(F32).astype(BF16)
         for low in range(0, ni, PLANES):
-            at = low + REACH
-            here = slice(at, at + PLANES)
-            centre = cur[here, SIDE:SIDE + nc, :]
-            high_part, low_part = halves(centre.reshape(part, nz))
-            total = mul(jnp.concatenate([high_part, low_part], axis=1), main)
-            total = total + mul(
-                jnp.concatenate([high_part, q[low * nc:low * nc + part, :]], axis=1), side
-            )
-            total = total.reshape(PLANES, nc, nz)
-            for k in range(1, 5):
-                around = (
-                    cur[at + k:at + k + PLANES, SIDE:SIDE + nc, :]
-                    + cur[at - k:at - k + PLANES, SIDE:SIDE + nc, :]
-                ) + (cur[here, SIDE + k:SIDE + k + nc, :] + cur[here, SIDE - k:SIDE - k + nc, :])
-                total = total + COEFFS[k] * around
-            fresh = 2.0 * centre - new[here, SIDE:SIDE + nc, :] + speed[low:low + PLANES] * total
-            new[here, SIDE:SIDE + nc, :] = fresh
-            if field == 1:
-                corr[low:low + PLANES] += fresh * s_at(slot)[here, SIDE:SIDE + nc, :]
-
-    def s_at(slot):
-        return fields[0][1 - slot]
+            at, row = low + REACH, low * nc
+            high_part, low_part = halves(cur[at:at + PLANES, SIDE:SIDE + nc, :].reshape(part, nz))
+            factors[field, row:row + part, 0:nz] = high_part
+            factors[field, row:row + part, nz:2 * nz] = low_part
+            factors[field, row:row + part, 2 * nz:3 * nz] = high_part
+        product[...] = jnp.dot(factors[field], weight[field], preferred_element_type=F32)
+        for low in range(0, ni, PLANES):
+            at, row = low + REACH, low * nc
+            here = (slice(at, at + PLANES), slice(SIDE, SIDE + nc))
+            centre = cur[here]
+            total = product[row:row + part, :].reshape(PLANES, nc, nz) + (3.0 * COEFFS[0]) * centre
+            new[here] = (2.0 * centre - new[here]) + speed[low:low + PLANES] * total
+
+    def update(field, slot, low, count, col):
+        cur, new = fields[field][slot], fields[field][1 - slot]
+        at, side = low + REACH, SIDE + col
+        window = cur[low:low + count + 2 * REACH, side:side + 8, :]
+        total = None
+        for k in range(1, 5):
+            around = (
+                window[REACH + k:REACH + k + count] + window[REACH - k:REACH - k + count]
+            ) + (cur[at:at + count, side + k:side + k + 8, :] + cur[at:at + count, side - k:side - k + 8, :])
+            total = COEFFS[k] * around if total is None else total + COEFFS[k] * around
+        here = (slice(at, at + count), slice(side, side + 8))
+        new[here] = new[here] + speed[low:low + count, col:col + 8, :] * total
+
+    def column(field, slot, col):
+        for low in range(REACH, ni - REACH, 8):
+            update(field, slot, low, 8, col)
+
+    def edges(field, slot):
+        @pl.when(left)
+        def _():
+            column(field, slot, 0)
+        @pl.when(right)
+        def _():
+            column(field, slot, nc - 8)
+        for low in (0, ni - REACH):
+            for col in range(0, nc, 8):
+                update(field, slot, low, REACH, col)
+
+    def middle(field, slot):
+        @pl.when(jnp.logical_not(left))
+        def _():
+            column(field, slot, 0)
+        @pl.when(jnp.logical_not(right))
+        def _():
+            column(field, slot, nc - 8)
+        for col in range(8, nc - 8, 8):
+            column(field, slot, col)
+
+    def correlate(slot):
+        for low in range(0, ni, PLANES):
+            here = (slice(low + REACH, low + REACH + PLANES), slice(SIDE, SIDE + nc))
+            corr[low:low + PLANES] += fields[0][slot][here] * fields[1][slot][here]
+
+    depth(0, 0, 0)
+    depth(1, 0, 0)
 
     @pl.loop(0, STEPS // 2)
     def _(pair):
+        more = pair < STEPS // 2 - 1
         for slot in range(2):
+            moment = 2 * pair + slot
             for field in range(2):
                 receive(field, slot)
-                if slot == 0:
-                    @pl.when(pair > 0)
-                    def _():
-                        sent(field, 1)
-                else:
-                    sent(field, 0)
-                advance(field, slot, 2 * pair + slot)
+                edges(field, slot)
                 if slot == 0:
                     send(field, 1)
                 else:
-                    @pl.when(pair < STEPS // 2 - 1)
+                    @pl.when(more)
                     def _():
                         send(field, 0)
+            for field in range(2):
+                middle(field, slot)
+                sent(field, slot)
+                if slot == 0:
+                    depth(field, 1, moment + 1)
+                else:
+                    @pl.when(more)
+                    def _():
+                        depth(field, 0, moment + 1)
+            correlate(1 - slot)
 
     theirs = pl.ds((1 - sa) * half, half)
     own = pl.ds(sa * half, half)
@@ -250,8 +290,6 @@
     ]
     for store in stores:
         store.start()
-    sent(0, 1)
-    sent(1, 1)
     swap.wait()
     mine[...] = (corr[own] + other[...]) * (1.0 / STEPS)
     last = pltpu.make_async_copy(mine, image, store_sem.at[4])
@@ -261,11 +299,19 @@
     last.wait()
 
 
+def leave(*refs):
+    copies = [pltpu.make_async_copy(refs[n], refs[5 + n], refs[10].at[n]) for n in range(5)]
+    for copy in copies:
+        copy.start()
+    for copy in copies:
+        copy.wait()
+
+
 def body(s_now, s_later, r_now, r_later, courant, wave, traces, s_in, s_cr, r_in, r_cr):
     ni, nc, nz = courant.shape
     half = ni // 2
     wide = (ni + 2 * REACH, nc + 2 * SIDE, nz)
-    hbm = pl.BlockSpec(memory_space=pl.ANY)
+    hbm = pl.BlockSpec(memory_space=pltpu.HBM)
     vmem = pl.BlockSpec(memory_space=pltpu.VMEM)
     smem = pl.BlockSpec(memory_space=pltpu.SMEM)
     tile = jax.ShapeDtypeStruct((ni, nc, nz), F32)
@@ -273,17 +319,17 @@
         kernel,
         out_shape=[tile] * 4 + [jax.ShapeDtypeStruct((half, nc, nz), F32)],
         in_specs=[hbm] * 5 + [vmem] * 2 + [smem] * 2 + [vmem] * 2,
-        out_specs=[hbm] * 5,
+        out_specs=[pl.BlockSpec(memory_space=pl.ANY)] * 5,
         scratch_shapes=[pltpu.VMEM(wide, F32)] * 4
         + [
             pltpu.VMEM((ni, nc, nz), F32),
             pltpu.VMEM((ni, nc, nz), F32),
             pltpu.VMEM((half, nc, nz), F32),
             pltpu.VMEM((half, nc, nz), F32),
-            pltpu.VMEM((ni * nc, nz), BF16),
-            pltpu.VMEM((ni * nc, nz), BF16),
-            pltpu.VMEM((2 * nz, nz), BF16),
-            pltpu.VMEM((2, 2 * nz, nz), BF16),
+            pltpu.VMEM((2, ni * nc, 4 * nz), BF16),
+            pltpu.VMEM((2, 4 * nz, nz), BF16),
+            pltpu.VMEM((ni * nc, nz), F32),
+            pltpu.VMEM((STEPS, traces.shape[2]), F32),
             pltpu.VMEM((2, 2, 2, ni, REACH, nz), F32),
             pltpu.VMEM((2, 2, 2, ni, REACH, nz), F32),
             pltpu.SemaphoreType.DMA((5,)),
@@ -293,10 +339,18 @@
             pltpu.SemaphoreType.DMA((5,)),
         ],
         compiler_params=pltpu.CompilerParams(
-            collective_id=0, has_side_effects=True, vmem_limit_bytes=62 * 1024 * 1024
+            collective_id=0, has_side_effects=True, vmem_limit_bytes=32 * 1024 * 1024
         ),
         name="window",
-    )(s_now[0], s_later[0], r_now[0], r_later[0], courant, wave, traces, s_in, s_cr, r_in, r_cr)
+    )(s_now[0], s_later[0], r_now[0], r_later[0], courant, wave, jnp.transpose(traces, (1, 0, 2)), s_in, s_cr, r_in, r_cr)
+    outs = pl.pallas_call(
+        leave,
+        out_shape=[jax.ShapeDtypeStruct(out.shape, F32) for out in outs],
+        in_specs=[pl.BlockSpec(memory_space=pl.ANY)] * 5,
+        out_specs=[hbm] * 5,
+        scratch_shapes=[pltpu.SemaphoreType.DMA((5,))],
+        name="leave",
+    )(*outs)
     return tuple(out[None] for out in outs[:4]) + (outs[4],)
 
 

time: 67.5 us -> 119 us (1.76)
  Pallas kernels: 58.8 us -> 107 us
  local copies, waits for them, and re-layouts: 6.44 us -> 9.31 us
    pallas_call x0 -> x1, Pallas kernels: none -> 54.7 us  [body(): pl.pallas_call(leave, out_shape=[jax.ShapeDtypeStruct(out.shape, F32) for...]
    pallas_call x1, Pallas kernels: 58.8 us -> 52.5 us  [body(): pl.pallas_call(kernel, out_shape=[tile] * 4 + [jax.ShapeDtypeStruct((half...]
    unnamed x16 -> x28, local copies, waits for them, and re-layouts: 6.44 us -> 9.31 us
where the time goes in v1:
time: 119 us
  Pallas kernels  107 us (90%)
  local copies, waits for them, and re-layouts  9.31 us (8%)
  between operations  2.01 us (2%)
    pallas_call x1, Pallas kernels, body(): pl.pallas_call(leave, out_shape=[jax.ShapeDtypeStruct(out.shape, F32) for...  54.7 us
    pallas_call x1, Pallas kernels, body(): pl.pallas_call(kernel, out_shape=[tile] * 4 + [jax.ShapeDtypeStruct((half...  52.5 us
    unnamed x28, local copies, waits for them, and re-layouts  9.31 us

profile of v1, /device:TPU:0, one launch (start us, length us, event | category | flops | bytes accessed | tf_op | source)
XLA Modules:
  0.0 118.6 jit_solution(2162779728935940653)
XLA Ops:
  1.3 0.0 copy-start.10
  1.9 0.0 copy-start.11
  2.0 0.0 copy-start.12
  2.0 0.0 copy-start.13
  2.0 0.0 copy-done.10
  2.0 0.6 copy-done.11
  2.6 0.0 copy-done.12
  2.6 0.0 copy-done.13
  2.6 0.0 copy-start.4
  2.6 1.0 copy-done.4
  3.6 0.0 copy-start.5
  3.6 1.0 copy-done.5
  4.6 0.0 copy-start.6
  4.6 1.0 copy-done.6
  5.6 0.0 copy-start.7
  5.6 1.0 copy-done.7
  6.6 0.0 copy-start.8
  6.6 1.0 copy-done.8
  7.6 52.5 %window.1 = (f32[32,24,128]{2,1,0:T(8,128)S(1)}, f32[32,24,128]{2,1,0:T(8,128)S(1)}, f32[32,24,128]{2,1,0:T(8,128)S(1)}, f32[32,24,128]{2,1,0:T(8,128)S(1)}, f32[16,24,128]{2,1,0:T(8,128)S(1)}) custom-call(f32[32,24,128]{2,1,0:T(8,128)S(1)} %bitcast.9, f32[32,24,128]{2,1,0:T(8,128)S(1)} %bitcast.10, f32[32,24,128]{2,1,0:T(8,128)S(1)} %bitcast.11, ...), custom_call_target="tpu_custom_call" | custom-call | tf_op jit(solution)/shard_map/window/pallas_call | solution.py:318
  60.1 0.0 copy-start
  60.1 0.7 copy-done
  60.9 0.0 copy-start.1
  60.9 0.8 copy-done.1
  61.6 0.0 copy-start.2
  61.6 0.7 copy-done.2
  62.4 0.0 copy-start.3
  62.4 0.8 copy-done.3
  63.1 0.0 copy-start.9
  63.1 0.7 copy-done.9
  63.8 54.7 %leave.1 = (f32[32,24,128]{2,1,0:T(8,128)}, f32[32,24,128]{2,1,0:T(8,128)}, f32[32,24,128]{2,1,0:T(8,128)}, f32[32,24,128]{2,1,0:T(8,128)}, f32[16,24,128]{2,1,0:T(8,128)}) custom-call(f32[32,24,128]{2,1,0:T(8,128)} %copy-done, f32[32,24,128]{2,1,0:T(8,128)} %copy-done.1, f32[32,24,128]{2,1,0:T(8,128)} %copy-done.2, f32[32,24,128]{2,1,0:T(8,128)} %copy-done.3, ...), custom_call_target="tpu_custom_call" | custom-call | tf_op jit(solution)/shard_map/leave/pallas_call | solution.py:346
Async XLA Ops:
  1.3 0.7 copy-start.10
  1.9 0.7 copy-start.11
  2.0 0.7 copy-start.12
  2.0 0.7 copy-start.13
  2.6 1.0 copy-start.4
  3.6 1.0 copy-start.5
  4.6 1.0 copy-start.6
  5.6 1.0 copy-start.7
  6.6 1.0 copy-start.8
  60.1 0.7 copy-start
  60.9 0.8 copy-start.1
  61.6 0.7 copy-start.2
  62.4 0.8 copy-start.3
  63.1 0.7 copy-start.9

commit v2 on v1

--- a/solution.py
+++ b/solution.py
@@ -300,11 +300,16 @@
 
 
 def leave(*refs):
-    copies = [pltpu.make_async_copy(refs[n], refs[5 + n], refs[10].at[n]) for n in range(5)]
-    for copy in copies:
-        copy.start()
-    for copy in copies:
-        copy.wait()
+    sems = refs[15]
+    loads = [pltpu.make_async_copy(refs[n], refs[10 + n], sems.at[0, n]) for n in range(5)]
+    stores = [pltpu.make_async_copy(refs[10 + n], refs[5 + n], sems.at[1, n]) for n in range(5)]
+    for load in loads:
+        load.start()
+    for load, store in zip(loads, stores):
+        load.wait()
+        store.start()
+    for store in stores:
+        store.wait()
 
 
 def body(s_now, s_later, r_now, r_later, courant, wave, traces, s_in, s_cr, r_in, r_cr):
@@ -339,7 +344,7 @@
             pltpu.SemaphoreType.DMA((5,)),
         ],
         compiler_params=pltpu.CompilerParams(
-            collective_id=0, has_side_effects=True, vmem_limit_bytes=32 * 1024 * 1024
+            collective_id=0, has_side_effects=True, vmem_limit_bytes=62 * 1024 * 1024
         ),
         name="window",
     )(s_now[0], s_later[0], r_now[0], r_later[0], courant, wave, jnp.transpose(traces, (1, 0, 2)), s_in, s_cr, r_in, r_cr)
@@ -348,7 +353,8 @@
         out_shape=[jax.ShapeDtypeStruct(out.shape, F32) for out in outs],
         in_specs=[pl.BlockSpec(memory_space=pl.ANY)] * 5,
         out_specs=[hbm] * 5,
-        scratch_shapes=[pltpu.SemaphoreType.DMA((5,))],
+        scratch_shapes=[pltpu.VMEM(out.shape, F32) for out in outs] + [pltpu.SemaphoreType.DMA((2, 5))],
+        compiler_params=pltpu.CompilerParams(vmem_limit_bytes=62 * 1024 * 1024),
         name="leave",
     )(*outs)
     return tuple(out[None] for out in outs[:4]) + (outs[4],)

time: 119 us -> 58.2 us (0.49)
  Pallas kernels: 107 us -> 56 us
  local copies, waits for them, and re-layouts: 9.31 us -> 0 us
    pallas_call x1, Pallas kernels: 54.7 us -> 2.28 us  [body(): pl.pallas_call(leave, out_shape=[jax.ShapeDtypeStruct(out.shape, F32) for...]
    unnamed x28 -> x0, local copies, waits for them, and re-layouts: 9.31 us -> none
    pallas_call x1, Pallas kernels: 52.5 us -> 53.7 us  [body(): pl.pallas_call(kernel, out_shape=[tile] * 4 + [jax.ShapeDtypeStruct((half...]
where the time goes in v2:
time: 58.2 us; the launch traced here: 57.9 us
  Pallas kernels  56 us (96%)
  between operations  1.93 us (3%)
    pallas_call x1, Pallas kernels, body(): pl.pallas_call(kernel, out_shape=[tile] * 4 + [jax.ShapeDtypeStruct((half...  53.7 us
    pallas_call x1, Pallas kernels, body(): pl.pallas_call(leave, out_shape=[jax.ShapeDtypeStruct(out.shape, F32) for...  2.28 us

profile of v2, /device:TPU:0, one launch (start us, length us, event | category | flops | bytes accessed | tf_op | source)
XLA Modules:
  0.0 57.9 jit_solution(11732351206293125711)
XLA Ops:
  1.9 53.7 %window.1 = (f32[32,24,128]{2,1,0:T(8,128)}, f32[32,24,128]{2,1,0:T(8,128)}, f32[32,24,128]{2,1,0:T(8,128)}, f32[32,24,128]{2,1,0:T(8,128)}, f32[16,24,128]{2,1,0:T(8,128)}) custom-call(f32[32,24,128]{2,1,0:T(8,128)} %bitcast.9, f32[32,24,128]{2,1,0:T(8,128)} %bitcast.10, f32[32,24,128]{2,1,0:T(8,128)} %bitcast.11, f32[32,24,128]{2,1,0:T(8,128)} %bitcast.12, ...), custom_call_target="tpu_custom_call" | custom-call | tf_op jit(solution)/shard_map/window/pallas_call | solution.py:323
  55.7 2.3 %leave.1 = (f32[32,24,128]{2,1,0:T(8,128)}, f32[32,24,128]{2,1,0:T(8,128)}, f32[32,24,128]{2,1,0:T(8,128)}, f32[32,24,128]{2,1,0:T(8,128)}, f32[16,24,128]{2,1,0:T(8,128)}) custom-call(f32[32,24,128]{2,1,0:T(8,128)} %get-tuple-element.15.refs_0_, f32[32,24,128]{2,1,0:T(8,128)} %get-tuple-element.16.refs_1_, f32[32,24,128]{2,1,0:T(8,128)} %get-tuple-element.17.refs_2_, ...), custom_call_target="tpu_custom_call" | custom-call | tf_op jit(solution)/shard_map/leave/pallas_call | solution.py:351

commit v3 on v2

--- a/solution.py
+++ b/solution.py
@@ -30,7 +30,7 @@
     s_now, s_later, r_now, r_later, speed_in,
     wave, traces, s_in, s_cr, r_in, r_cr,
     s_first, s_second, r_first, r_second, image,
-    s0, s1, r0, r1, speed, corr, other, mine, factors, weight, product, records,
+    s0, s1, r0, r1, speed, corr, other, mine, factors, weight, product, cross_table, records,
     x_out, x_in, load_sem, send_sem, recv_sem, sum_sem, store_sem,
 ):
     ni, nc, nz = speed.shape
@@ -187,6 +187,19 @@
     for load in loads[2:]:
         load.wait()
 
+    spare = -3 * nc % 16
+    to = lax.broadcasted_iota(jnp.int32, (nc, 3 * nc + spare), 0)
+    of = lax.broadcasted_iota(jnp.int32, (nc, 3 * nc + spare), 1)
+    cross = jnp.zeros((nc, 3 * nc + spare), F32)
+    for distance in range(1, 5):
+        cross = jnp.where(jnp.abs(to - of % nc) == distance, COEFFS[distance], cross)
+    cross_high = cross.astype(BF16).astype(F32)
+    group = of // nc
+    cross_table[...] = jnp.where(
+        group < 2, cross_high, jnp.where(group == 2, cross - cross_high, 0.0)
+    ).astype(BF16)
+    fill = [jnp.zeros((spare, nz), F32)] if spare else []
+
     def depth(field, slot, moment):
         cur, new = fields[field][slot], fields[field][1 - slot]
         level = (SRC_DEPTH, REC_DEPTH)[field]
@@ -198,23 +211,40 @@
             factors[field, row:row + part, 0:nz] = high_part
             factors[field, row:row + part, nz:2 * nz] = low_part
             factors[field, row:row + part, 2 * nz:3 * nz] = high_part
+        cross_band = cross_table[...]
         product[...] = jnp.dot(factors[field], weight[field], preferred_element_type=F32)
         for low in range(0, ni, PLANES):
             at, row = low + REACH, low * nc
             here = (slice(at, at + PLANES), slice(SIDE, SIDE + nc))
             centre = cur[here]
+            first = centre.astype(BF16).astype(F32)
+            rest = centre - first
+            across = []
+            for p in range(0, PLANES, 2):
+                stacks = [
+                    jnp.concatenate([first[p + n], rest[p + n], first[p + n]] + fill, axis=0)
+                    for n in range(2)
+                ]
+                both = jnp.dot(
+                    cross_band, jnp.concatenate(stacks, axis=1).astype(BF16), preferred_element_type=F32
+                )
+                across += [both[:, :nz], both[:, nz:]]
             total = product[row:row + part, :].reshape(PLANES, nc, nz) + (3.0 * COEFFS[0]) * centre
+            total = total + jnp.stack(across)
             new[here] = (2.0 * centre - new[here]) + speed[low:low + PLANES] * total
 
     def update(field, slot, low, count, col):
         cur, new = fields[field][slot], fields[field][1 - slot]
         at, side = low + REACH, SIDE + col
         window = cur[low:low + count + 2 * REACH, side:side + 8, :]
+        row = lax.broadcasted_iota(jnp.int32, (count, 8, nz), 1)
         total = None
         for k in range(1, 5):
-            around = (
-                window[REACH + k:REACH + k + count] + window[REACH - k:REACH - k + count]
-            ) + (cur[at:at + count, side + k:side + k + 8, :] + cur[at:at + count, side - k:side - k + 8, :])
+            around = window[REACH + k:REACH + k + count] + window[REACH - k:REACH - k + count]
+            if col == 0:
+                around = around + jnp.where(row < k, cur[at:at + count, side - k:side - k + 8, :], 0.0)
+            if col == nc - 8:
+                around = around + jnp.where(row >= 8 - k, cur[at:at + count, side + k:side + k + 8, :], 0.0)
             total = COEFFS[k] * around if total is None else total + COEFFS[k] * around
         here = (slice(at, at + count), slice(side, side + 8))
         new[here] = new[here] + speed[low:low + count, col:col + 8, :] * total
@@ -334,6 +364,7 @@
             pltpu.VMEM((2, ni * nc, 4 * nz), BF16),
             pltpu.VMEM((2, 4 * nz, nz), BF16),
             pltpu.VMEM((ni * nc, nz), F32),
+            pltpu.VMEM((nc, 3 * nc + -3 * nc % 16), BF16),
             pltpu.VMEM((STEPS, traces.shape[2]), F32),
             pltpu.VMEM((2, 2, 2, ni, REACH, nz), F32),
             pltpu.VMEM((2, 2, 2, ni, REACH, nz), F32),

time: 58.2 us -> 58.2 us (level)
  no operation moved by 1% of the time
where the time goes in v3:
time: 58.2 us; the launch traced here: 57.9 us
  Pallas kernels  56 us (96%)
  between operations  1.93 us (3%)
    pallas_call x1, Pallas kernels, body(): pl.pallas_call(kernel, out_shape=[tile] * 4 + [jax.ShapeDtypeStruct((half...  53.7 us
    pallas_call x1, Pallas kernels, body(): pl.pallas_call(leave, out_shape=[jax.ShapeDtypeStruct(out.shape, F32) for...  2.28 us

profile of v3, /device:TPU:0, one launch (start us, length us, event | category | flops | bytes accessed | tf_op | source)
XLA Modules:
  0.0 57.9 jit_solution(11404733854267187428)
XLA Ops:
  1.9 53.7 %window.1 = (f32[32,24,128]{2,1,0:T(8,128)}, f32[32,24,128]{2,1,0:T(8,128)}, f32[32,24,128]{2,1,0:T(8,128)}, f32[32,24,128]{2,1,0:T(8,128)}, f32[16,24,128]{2,1,0:T(8,128)}) custom-call(f32[32,24,128]{2,1,0:T(8,128)} %bitcast.9, f32[32,24,128]{2,1,0:T(8,128)} %bitcast.10, f32[32,24,128]{2,1,0:T(8,128)} %bitcast.11, f32[32,24,128]{2,1,0:T(8,128)} %bitcast.12, ...), custom_call_target="tpu_custom_call" | custom-call | tf_op jit(solution)/shard_map/window/pallas_call | solution.py:353
  55.7 2.3 %leave.1 = (f32[32,24,128]{2,1,0:T(8,128)}, f32[32,24,128]{2,1,0:T(8,128)}, f32[32,24,128]{2,1,0:T(8,128)}, f32[32,24,128]{2,1,0:T(8,128)}, f32[16,24,128]{2,1,0:T(8,128)}) custom-call(f32[32,24,128]{2,1,0:T(8,128)} %get-tuple-element.15.refs_0_, f32[32,24,128]{2,1,0:T(8,128)} %get-tuple-element.16.refs_1_, f32[32,24,128]{2,1,0:T(8,128)} %get-tuple-element.17.refs_2_, ...), custom_call_target="tpu_custom_call" | custom-call | tf_op jit(solution)/shard_map/leave/pallas_call | solution.py:382
